TPU v7x, 32 devices: a whole 2x2x4 slice. The times are simulated.
32 devices in a mesh: sens: 4 (over y, core), tm: 8 (over z, x).
Axes of the slice: x: 2, y: 2, z: 4, core: 2. Of those that a mesh axis runs over, the one named last changes fastest.
Arguments:
- observations: bfloat16 [65536, 2048], P('sens', 'tm'), may hold values from -6 to 6
- loadings: float32 [65536, 128], P('sens'), may hold values from -6 to 6
- noise_var: float32 [65536], P('sens'), may hold values from 0.25 to 4
- decay: float32 [2048, 128], P('tm'), may hold values from 0.4 to 1
- tiles: int32 [3072, 2], replicated, may hold values from 0 to 511, as said below
Outputs:
- new_loadings: float32 [65536, 128], P(('sens', 'tm'))
- new_noise: float32 [65536], P(('sens', 'tm'))
Inputs may be any that keep to these rules, and one draw needn't show every extreme that they name: `tiles`: every pair is a distinct tile; every sensor block appears in at least one pair; the second entry is below 8.
All inputs are finite; a program needn't handle non-finite values.
Results may differ from a plain program's by a relative error of at most 0.0059.
Values may be sent and summed in bfloat16 or wider, within the bound.
A program may use at most 128 MiB of HBM per device.

v0:
```python
import jax
import jax.numpy as jnp
from jax import lax
from jax.sharding import PartitionSpec as P

BLOCK = 128


HIGH = lax.Precision.HIGHEST


def carried_in(part, axis, combine, identity, reverse):
    count = lax.axis_size(axis)
    place = lax.axis_index(axis)
    ahead = count - 1 - place if reverse else place
    gathered = jax.tree.map(lambda a: lax.all_gather(a, axis), part)
    state = jax.tree.map(lambda a, e: jnp.zeros_like(a) + jnp.asarray(e, a.dtype), part, identity)

    def one(step, state):
        source = count - 1 - step if reverse else step
        return combine(
            state, jax.tree.map(lambda a: lax.dynamic_index_in_dim(a, source, 0, False), gathered)
        )

    return lax.fori_loop(0, ahead, one, state)


def compose(before_seg, after_seg):
    return (before_seg[0] * after_seg[0], after_seg[0] * before_seg[1] + after_seg[1])


def prefix_rows(gains, values, position):
    inclusive = lax.associative_scan(compose, (gains, values), axis=0)
    shifted_gain = jnp.concatenate([jnp.ones_like(gains[:1]), inclusive[0][:-1]], 0)
    shifted_value = jnp.concatenate([jnp.zeros_like(values[:1]), inclusive[1][:-1]], 0)
    before_gain = lax.dynamic_index_in_dim(shifted_gain, position, 0, keepdims=True)
    before_value = lax.dynamic_index_in_dim(shifted_value, position, 0, keepdims=True)
    return ((before_gain, before_value), (inclusive[0][-1:], inclusive[1][-1:]))


def per_device(observations, loadings, noise_var, decay, tiles):
    sens_count = lax.axis_size("sens")
    time_count = lax.axis_size("tm")
    sens_index = lax.axis_index("sens")
    time_index = lax.axis_index("tm")
    sens_dev, window_len = observations.shape
    factors = loadings.shape[1]
    blocks_dev = sens_dev // BLOCK
    blocks_share = blocks_dev // time_count
    segment_len = window_len // sens_count
    block_ids = sens_index * blocks_dev + jnp.arange(blocks_dev)
    block_hit = (tiles[:, 0][:, None] == block_ids[None, :]).astype(jnp.float32)
    window_hit = (tiles[:, 1][:, None] == jnp.arange(time_count)[None, :]).astype(jnp.float32)
    tile_mask = jnp.dot(block_hit.T, window_hit, precision=HIGH)
    present = lax.dynamic_index_in_dim(tile_mask, time_index, 1, keepdims=False)
    sensor_mask = jnp.repeat(present, BLOCK)
    weighted = loadings / noise_var[:, None] * sensor_mask[:, None]
    scaled = weighted.astype(jnp.bfloat16)
    info_part = lax.dot_general(
        observations, scaled, (((0,), (0,)), ((), ())), preferred_element_type=jnp.float32
    )
    gram_part = jnp.dot(weighted.T, loadings, precision=HIGH)
    info_vec = lax.psum_scatter(info_part, "sens", scatter_dimension=0, tiled=True)
    information = lax.psum(gram_part, "sens")
    identity = jnp.eye(factors, dtype=jnp.float32)
    lower = jnp.linalg.cholesky(identity + information)
    covariance = jax.scipy.linalg.cho_solve((lower, True), identity)
    local_est = jnp.dot(info_vec, covariance, precision=HIGH)
    decays = lax.dynamic_slice_in_dim(decay, sens_index * segment_len, segment_len, 0)
    fwd_gain, fwd_local = lax.associative_scan(compose, (decays, local_est), axis=0)
    back_gain, back_local = lax.associative_scan(
        compose, (jnp.flip(decays, 0), jnp.flip(local_est, 0)), axis=0
    )
    members = (
        lax.all_gather(fwd_gain[-1:], "sens", axis=0, tiled=True),
        lax.all_gather(fwd_local[-1:], "sens", axis=0, tiled=True),
        lax.all_gather(back_gain[-1:], "sens", axis=0, tiled=True),
        lax.all_gather(back_local[-1:], "sens", axis=0, tiled=True),
    )
    back_gain = jnp.flip(back_gain, 0)
    back_local = jnp.flip(back_local, 0)
    sens_fwd, group_fwd = prefix_rows(members[0], members[1], sens_index)
    sens_back, group_back = prefix_rows(
        jnp.flip(members[2], 0), jnp.flip(members[3], 0), sens_count - 1 - sens_index
    )
    time_fwd = carried_in(
        (group_fwd[0], group_fwd[1]),
        "tm",
        compose,
        (jnp.ones_like(group_fwd[0]), jnp.zeros_like(group_fwd[1])),
        False,
    )
    time_back = carried_in(
        (group_back[0], group_back[1]),
        "tm",
        compose,
        (jnp.ones_like(group_back[0]), jnp.zeros_like(group_back[1])),
        True,
    )
    enter_fwd = compose(time_fwd, sens_fwd)[1]
    enter_back = compose(time_back, sens_back)[1]
    forward = fwd_local + fwd_gain * enter_fwd
    backward = back_local + back_gain * enter_back
    smoothed = ((1.0 - decays) / (1.0 + decays) * (forward + backward - local_est)).astype(
        jnp.bfloat16
    )
    mask_mine = lax.dynamic_slice_in_dim(tile_mask, time_index * blocks_share, blocks_share, 0)
    observed = observations * sensor_mask.astype(jnp.bfloat16)[:, None]
    sums_sq = jnp.sum(jnp.square(observed.astype(jnp.float32)), axis=1)
    shard_rows = lax.all_gather(smoothed, "sens", axis=0, tiled=True)
    cross_terms = jnp.dot(observed, shard_rows, preferred_element_type=jnp.float32)
    squares = lax.dot_general(
        shard_rows, shard_rows, (((0,), (0,)), ((), ())), preferred_element_type=jnp.float32
    )
    cross_terms, squares = (cross_terms, squares)
    moment = squares + window_len * covariance
    cross_mine, sq_mine = (
        lax.psum_scatter(cross_terms, "tm", scatter_dimension=0, tiled=True),
        lax.psum_scatter(sums_sq, "tm", scatter_dimension=0, tiled=True),
    )
    all_moments = lax.all_gather(moment[None], "tm", axis=0, tiled=True)
    moment_mine = jnp.einsum("bw,wij->bij", mask_mine, all_moments, precision=HIGH)
    counts_mine = jnp.sum(mask_mine, axis=1)
    cross_blocks = cross_mine.reshape(blocks_share, BLOCK, factors)

    def solve_block(moment_block, cross_block):
        lower_block = jnp.linalg.cholesky(moment_block)
        return jax.scipy.linalg.cho_solve((lower_block, True), cross_block.T).T

    new_loadings = jax.vmap(solve_block)(moment_mine, cross_blocks).reshape(
        blocks_share * BLOCK, factors
    )
    explained = jnp.sum(new_loadings * cross_mine, axis=1)
    new_noise = (sq_mine - explained) / (window_len * jnp.repeat(counts_mine, BLOCK))
    return (new_loadings, new_noise)


def solution(mesh):
    return jax.shard_map(
        per_device,
        mesh=mesh,
        in_specs=(P("sens", "tm"), P("sens", None), P("sens"), P("tm", None), P()),
        out_specs=(P(("sens", "tm"), None), P(("sens", "tm"))),
        check_vma=False,
    )
```

profile of v0, /device:TPU:0, one launch (start us, length us, event | category | flops | bytes accessed | tf_op | source)
XLA Modules:
  0.0 606.7 jit_solution(7031765170658476575)
XLA Ops:
  7.2 0.0 all-reduce.72.cloned.1.call-start
  7.2 0.8 fusion.48
  8.1 0.6 fusion.9
  8.7 0.1 broadcast_bitcast_fusion
  8.7 0.0 copy-start.2
  8.8 25.1 %fusion.2 = f32[128,128]{1,0:T(8,128)} fusion(f32[16384,128]{1,0:T(8,128)} %param.10, f32[16384]{0:T(1024)S(1)} %broadcast_bitcast_fusion, f32[16384]{0:T(1024)} %param.11), kind=kOutput, calls=%fused_computation.8 | convolution fusion | flops 3225419776 | bytes 8585216 | tf_op jit(solution)/shard_map/dot_general | solution.py:62
  33.9 0.0 all-reduce.72.cloned.1.call-update
  33.9 0.0 copy-start.1
  33.9 0.0 reduce-scatter.7.cloned.1.call-start
  33.9 0.0 copy-done.2
  34.0 13.2 %fusion.11 = f32[256,128]{0,1:T(8,128)S(1)} fusion(bf16[16384,256]{1,0:T(8,128)(2,1)} %param.9, f32[16384,128]{1,0:T(8,128)} %param.10, f32[16384]{0:T(1024)S(1)} %broadcast_bitcast_fusion, f32[16384]{0:T(1024)S(1)} %copy-done.2), kind=kOutput, calls=%fused_computation.16 | convolution fusion | flops 1080033280 | bytes 17039360 | tf_op jit(solution)/shard_map/dot_general | solution.py:59
  47.2 0.8 copy.29
  47.9 0.0 reduce-scatter.7.cloned.1.call-update
  48.0 0.3 reduce-scatter.5.cloned.1.call-start
  48.2 0.0 copy-done.1
  48.3 0.1 bitcast_convert_fusion
  48.5 19.3 %all-reduce.72.cloned.1.call-done = f32[128,128]{1,0:T(8,128)} async-done(((f32[128,128]{1,0:T(8,128)}), f32[128,128]{1,0:T(8,128)}) %all-reduce.72.cloned.1.call-update) | async-done | bytes 65552 | tf_op jit(solution)/shard_map/psum | solution.py:64
  67.8 0.9 convert_add_fusion
  68.6 0.1 copy.19
  68.7 0.9 fusion.28
  69.6 11.7 %cholesky.32 = f32[128,128]{1,0:T(8,128)S(1)} custom-call(f32[128,128]{1,0:T(8,128)S(1)} %fusion.28), custom_call_target="Cholesky" | custom-call | tf_op jit(solution)/shard_map/jit(cholesky)/cholesky | solution.py:66
  81.3 0.7 compare_reduce_fusion.1
  82.1 0.7 fusion.23
  82.8 9.8 %custom-call.21 = f32[1,128,128]{1,2,0:T(8,128)S(1)} custom-call(f32[1,128,128]{2,1,0:T(8,128)S(1)} %fusion.23), custom_call_target="InvertDiagBlocksLowerTriangular" | custom-call | tf_op jit(solution)/shard_map/jit(_cho_solve)/triangular_solve | solution.py:67
  92.6 0.2 fusion.26
  92.8 0.2 fusion.24
  93.1 0.0 reduce-scatter.7.cloned.1.call-done
  93.1 0.9 fusion.58
  95.7 5.0 all-gather.9
  100.8 5.0 all-gather.11
  106.5 5.0 all-gather.5
  111.7 5.0 all-gather.7
  117.0 20.4 %all-gather.10 = f32[8,1,128]{2,1,0:T(1,128)S(1)} all-gather(f32[1,1,128]{2,1,0:T(1,128)S(1)} %slice_bitcast_fusion.9), channel_id=4, replica_groups=mesh['sens'=4,'tm'=8] {'tm'}, dimensions={0}, use_global_device_ids=true | all-gather | bytes 4608 | tf_op jit(solution)/shard_map/all_gather | solution.py:16
  137.5 16.2 %all-gather.12 = f32[8,1,128]{2,1,0:T(1,128)S(1)} all-gather(f32[1,1,128]{2,1,0:T(1,128)S(1)} %slice_bitcast_fusion.8), channel_id=5, replica_groups=mesh['sens'=4,'tm'=8] {'tm'}, dimensions={0}, use_global_device_ids=true | all-gather | bytes 4608 | tf_op jit(solution)/shard_map/all_gather | solution.py:16
  153.6 0.2 while.27
  154.0 18.1 %all-gather.6 = f32[8,1,128]{2,1,0:T(1,128)S(1)} all-gather(f32[1,1,128]{2,1,0:T(1,128)S(1)} %slice_bitcast_fusion.11), channel_id=2, replica_groups=mesh['sens'=4,'tm'=8] {'tm'}, dimensions={0}, use_global_device_ids=true | all-gather | bytes 4608 | tf_op jit(solution)/shard_map/all_gather | solution.py:16
  172.2 16.2 %all-gather.8 = f32[8,1,128]{2,1,0:T(1,128)S(1)} all-gather(f32[1,1,128]{2,1,0:T(1,128)S(1)} %slice_bitcast_fusion.10), channel_id=3, replica_groups=mesh['sens'=4,'tm'=8] {'tm'}, dimensions={0}, use_global_device_ids=true | all-gather | bytes 4608 | tf_op jit(solution)/shard_map/all_gather | solution.py:16
  188.4 5.2 all_gather.54
  193.7 6.8 %fusion = f32[16384,128]{1,0:T(8,128)} fusion(bf16[256,128]{1,0:T(8,128)(2,1)S(1)} %all_gather.54, bf16[16384,256]{1,0:T(8,128)(2,1)} %param.9, bf16[16384]{0:T(1024)(128)(2,1)S(1)} %bitcast_convert_fusion), kind=kOutput, calls=%fused_computation.6 | convolution fusion | flops 1077936128 | bytes 16875520 | tf_op jit(solution)/shard_map/dot_general | solution.py:111
  200.5 0.0 reduce-scatter.5.cloned.1.call-update
  200.5 0.0 all-reduce.74.cloned.1.call-start
  200.6 7.9 %multiply_reduce_fusion = f32[16384]{0:T(1024)} fusion(bf16[16384,256]{1,0:T(8,128)(2,1)} %param.9, bf16[16384]{0:T(1024)(128)(2,1)S(1)} %bitcast_convert_fusion), kind=kLoop, calls=%fused_computation.4 | loop fusion | flops 16760832 | bytes 8486912 | tf_op jit(solution)/shard_map/reduce_sum | solution.py:109
  208.4 0.0 all-reduce.74.cloned.1.call-update
  208.5 0.1 dynamic-slice_reduce_fusion
  208.6 0.0 copy-done.3
  208.6 0.6 dynamic-slice
  209.9 0.2 convolution_add_fusion
  210.1 34.4 %all-gather.4 = f32[1024,128]{1,0:T(8,128)S(1)} all-gather(f32[128,128]{1,0:T(8,128)S(1)} %convolution_add_fusion), channel_id=6, replica_groups=mesh['sens'=4,'tm'=8] {'tm'}, dimensions={0}, use_global_device_ids=true | all-gather | bytes 589824 | tf_op jit(solution)/shard_map/all_gather | solution.py:121
  244.5 1.2 fusion.21
  245.7 0.4 copy.21
  246.2 0.4 fusion.18
  246.6 187.5 %custom-call.22 = f32[16,128,128]{2,1,0:T(8,128)S(1)} custom-call(f32[16,128,128]{2,1,0:T(8,128)S(1)} %fusion.18), custom_call_target="Cholesky" | custom-call | tf_op jit(solution)/shard_map/vmap(jit(cholesky))/cholesky | solution.py:127
  434.1 0.1 select_reduce_fusion
  434.2 0.1 compare_reduce_fusion
  434.3 0.2 select_bitcast_fusion
  434.5 157.2 %custom-call.23 = f32[16,1,128,128]{2,3,1,0:T(8,128)S(1)} custom-call(f32[16,1,128,128]{3,2,1,0:T(8,128)S(1)} %select_bitcast_fusion), custom_call_target="InvertDiagBlocksLowerTriangular" | custom-call | tf_op jit(solution)/shard_map/vmap(jit(_cho_solve))/triangular_solve | solution.py:128
  591.7 0.0 reduce-scatter.5.cloned.1.call-done
  591.7 2.3 fusion.16
  594.0 2.3 fusion.14
  596.3 0.0 copy-start
  596.4 1.9 multiply_reduce_fusion.1
  598.3 0.0 all-reduce.74.cloned.1.call-done
  598.3 1.4 fusion.34
  599.7 0.0 copy-done
  (247 shorter events, 2.6 us)
Async XLA Ops:
  7.2 60.6 %all-reduce.72.cloned.1.call-start = ((), (), s32[]{:S(2)}) async-start(), calls=%async_computation.2 | async-start | bytes 131072 | tf_op jit(solution)/shard_map/psum | solution.py:64
  8.7 25.2 %copy-start.2 = (f32[16384]{0:T(1024)S(1)}, f32[16384]{0:T(1024)}, u32[]{:S(2)}) copy-start(f32[16384]{0:T(1024)} %param.11) | copy-start | bytes 196612
  33.9 14.3 %copy-start.1 = (f32[256,128]{1,0:T(8,128)S(1)}, f32[256,128]{1,0:T(8,128)}, u32[]{:S(2)}) copy-start(f32[256,128]{1,0:T(8,128)} %param.12) | copy-start | bytes 393220
  33.9 59.2 %reduce-scatter.7.cloned.1.call-start = ((), (), s32[]{:S(2)}) async-start(), calls=%async_computation.4 | async-start | bytes 163840
  48.0 543.7 %reduce-scatter.5.cloned.1.call-start = ((), (), s32[]{:S(2)}) async-start(), calls=%async_computation.3 | async-start | bytes 9437184 | tf_op jit(solution)/shard_map/reduce_scatter | solution.py:118
  200.5 8.1 %copy-start.3 = (u32[32]{0:T(128)S(1)}, u32[32]{0:T(128)}, u32[]{:S(2)}) copy-start(u32[32]{0:T(128)} %constant.324) | copy-start | bytes 388
  200.5 397.8 %all-reduce.74.cloned.1.call-start = ((), (), s32[]{:S(2)}) async-start(), calls=%async_computation.5 | async-start | bytes 131072
  596.3 3.4 copy-start
Sparse Core Ops, SparseCore 0:
  34.0 33.7 all-reduce.71
  70.9 19.7 reduce-scatter.6
  200.6 151.4 reduce-scatter.4
  355.7 68.7 all-reduce.73
where the time goes:
time: 616 us; the launch traced here: 607 us
  other arithmetic  382 us (62%)
  blocking collectives  131 us (21%)
  matrix products  53.1 us (9%)
  waiting for transfers between devices  19.4 us (3%)
  between operations  16 us (3%)
    another operation x4, other arithmetic, solve_block(): lower_block = jnp.linalg.cholesky(moment_block)  188 us
    another operation x3, other arithmetic, solve_block(): return jax.scipy.linalg.cho_solve((lower_block, True), cross_block.T).T  157 us
    all_gather x4, blocking collectives, carried_in(): gathered = jax.tree.map(lambda a: lax.all_gather(a, axis), part)  70.9 us
    all_gather x1, blocking collectives, per_device(): all_moments = lax.all_gather(moment[None], 'tm', axis=0, tiled=True)  34.4 us
    dot_general x1, matrix products, per_device(): gram_part = jnp.dot(weighted.T, loadings, precision=HIGH)  25.1 us
    psum x1, waiting for transfers between devices, per_device(): information = lax.psum(gram_part, 'sens')  19.3 us
    dot_general x1, matrix products, per_device(): lax.dot_general(observations, scaled, (((0,), (0,)), ((), ())), preferred...  13.2 us
    another operation x3, other arithmetic, per_device(): lower = jnp.linalg.cholesky(identity + information)  12.5 us
  transfers between devices with their start and end apart: 4, of which 1 were waited for; matrix products, arithmetic and copies ran while one was open for 66% of the time, Pallas kernels for 0%

commit v1 on v0

v1 whole, which is shorter than its diff:
```python
import functools

import jax
import jax.numpy as jnp
from jax import lax
from jax.experimental import pallas as pl
from jax.experimental.pallas import tpu as pltpu
from jax.sharding import PartitionSpec as P

BLOCK = 128
HIGH = lax.Precision.HIGHEST
F32 = jnp.float32
BF16 = jnp.bfloat16
TILE = 1024


def info_kernel(obs_ref, load_ref, rate_ref, out_ref):
    @pl.when(pl.program_id(0) == 0)
    def _():
        out_ref[...] = jnp.zeros_like(out_ref)

    load = load_ref[...]
    load_hi = load.astype(BF16)
    load_lo = (load - load_hi.astype(F32)).astype(BF16)
    weighted = load.T * rate_ref[...]
    hi = weighted.astype(BF16)
    lo = (weighted - hi.astype(F32)).astype(BF16)
    window = obs_ref.shape[1]
    right = jnp.concatenate([load_hi, load_lo], axis=1)
    factors = load.shape[1]
    out_ref[:, :window] += jnp.dot(hi, obs_ref[...], preferred_element_type=F32)
    both = jnp.dot(hi, right, preferred_element_type=F32)
    out_ref[:, window:] += (
        both[:, :factors] + both[:, factors:] + jnp.dot(lo, load_hi, preferred_element_type=F32)
    )


def info_and_gram(observations, loadings, rate):
    sensors, window = observations.shape
    factors = loadings.shape[1]
    return pl.pallas_call(
        info_kernel,
        grid=(sensors // TILE,),
        in_specs=[
            pl.BlockSpec((TILE, window), lambda i: (i, 0)),
            pl.BlockSpec((TILE, factors), lambda i: (i, 0)),
            pl.BlockSpec((1, TILE), lambda i: (0, i)),
        ],
        out_specs=pl.BlockSpec((factors, window + factors), lambda i: (0, 0)),
        out_shape=jax.ShapeDtypeStruct((factors, window + factors), F32),
        compiler_params=pltpu.CompilerParams(vmem_limit_bytes=40 * 2**20),
    )(observations, loadings, rate)


def invert_in_place(ref, count, size):
    lanes = lax.broadcasted_iota(jnp.int32, (1, size), 1)
    rows = lax.broadcasted_iota(jnp.int32, (size, 1), 0)

    def step(k, carry):
        lane = lanes == k
        sub = rows == k
        for b in range(count):
            a = ref[b]
            row = ref[b, pl.ds(k, 1), :]
            pivot = jnp.sum(jnp.where(lane, row, 0.0), axis=1, keepdims=True)
            scaled = jnp.where(lane, 1.0, row) / pivot
            col = jnp.sum(jnp.where(lane, a, 0.0), axis=1, keepdims=True)
            col = jnp.where(sub, -1.0, col)
            ref[b] = jnp.where(lane | sub, 0.0, a) - col * scaled
        return carry

    lax.fori_loop(0, size, step, 0)


def invert_kernel(a_ref, out_ref):
    out_ref[...] = a_ref[...]
    invert_in_place(out_ref, a_ref.shape[0], a_ref.shape[1])


def invert(a):
    return pl.pallas_call(
        invert_kernel,
        out_shape=jax.ShapeDtypeStruct(a.shape, F32),
        compiler_params=pltpu.CompilerParams(vmem_limit_bytes=40 * 2**20),
    )(a)


def compose(before_seg, after_seg):
    return (before_seg[0] * after_seg[0], after_seg[0] * before_seg[1] + after_seg[1])


def per_device(observations, loadings, noise_var, decay, tiles):
    time_count = lax.axis_size("tm")
    sens_index = lax.axis_index("sens")
    time_index = lax.axis_index("tm")
    sens_dev, window_len = observations.shape
    factors = loadings.shape[1]
    blocks_dev = sens_dev // BLOCK
    blocks_share = blocks_dev // time_count
    block_ids = sens_index * blocks_dev + jnp.arange(blocks_dev)
    block_hit = (tiles[:, 0][:, None] == block_ids[None, :]).astype(BF16)
    window_hit = (tiles[:, 1][:, None] == jnp.arange(time_count)[None, :]).astype(BF16)
    tile_mask = lax.dot_general(
        block_hit, window_hit, (((0,), (0,)), ((), ())), preferred_element_type=F32
    )
    present = lax.dynamic_index_in_dim(tile_mask, time_index, 1, keepdims=False)
    sensor_mask = jnp.repeat(present, BLOCK)
    rate = (sensor_mask / noise_var)[None, :]
    part = info_and_gram(observations, loadings, rate)
    total = lax.psum(part, "sens")
    identity = jnp.eye(factors, dtype=F32)
    covariance = invert((identity + total[:, window_len:])[None])[0]
    local_est = lax.dot_general(
        total[:, :window_len], covariance, (((0,), (0,)), ((), ())), precision=HIGH
    )
    fwd_gain, fwd_local = lax.associative_scan(compose, (decay, local_est), axis=0)
    back_gain, back_local = lax.associative_scan(
        compose, (jnp.flip(decay, 0), jnp.flip(local_est, 0)), axis=0
    )
    back_gain = jnp.flip(back_gain, 0)
    back_local = jnp.flip(back_local, 0)
    mine = jnp.stack([fwd_gain[-1], fwd_local[-1], back_local[0]])
    ends = lax.all_gather(mine, "tm")
    enter_fwd = jnp.zeros((factors,), F32)
    enter_back = jnp.zeros((factors,), F32)
    for w in range(time_count):
        step = ends[w, 0] * enter_fwd + ends[w, 1]
        enter_fwd = jnp.where(w < time_index, step, enter_fwd)
    for w in reversed(range(time_count)):
        step = ends[w, 0] * enter_back + ends[w, 2]
        enter_back = jnp.where(w > time_index, step, enter_back)
    forward = fwd_local + fwd_gain * enter_fwd
    backward = back_local + back_gain * enter_back
    smoothed = ((1.0 - decay) / (1.0 + decay) * (forward + backward - local_est)).astype(BF16)
    mask_mine = lax.dynamic_slice_in_dim(tile_mask, time_index * blocks_share, blocks_share, 0)
    observed = observations * sensor_mask.astype(BF16)[:, None]
    sums_sq = jnp.sum(jnp.square(observed.astype(F32)), axis=1)
    cross_terms = jnp.dot(observed, smoothed, preferred_element_type=F32)
    squares = lax.dot_general(
        smoothed, smoothed, (((0,), (0,)), ((), ())), preferred_element_type=F32
    )
    moment = squares + window_len * covariance
    cross_mine = lax.psum_scatter(cross_terms, "tm", scatter_dimension=0, tiled=True)
    sq_mine = lax.psum_scatter(sums_sq, "tm", scatter_dimension=0, tiled=True)
    all_moments = lax.all_gather(moment[None], "tm", axis=0, tiled=True)
    moment_mine = jnp.einsum("bw,wij->bij", mask_mine, all_moments, precision=HIGH)
    counts_mine = jnp.sum(mask_mine, axis=1)
    inverse = invert(moment_mine)
    cross_blocks = cross_mine.reshape(blocks_share, BLOCK, factors)
    new_loadings = jnp.einsum("bsf,bfg->bsg", cross_blocks, inverse, precision=HIGH).reshape(
        blocks_share * BLOCK, factors
    )
    explained = jnp.sum(new_loadings * cross_mine, axis=1)
    new_noise = (sq_mine - explained) / (window_len * jnp.repeat(counts_mine, BLOCK))
    return (new_loadings, new_noise)


def solution(mesh):
    return jax.shard_map(
        per_device,
        mesh=mesh,
        in_specs=(P("sens", "tm"), P("sens", None), P("sens"), P("tm", None), P()),
        out_specs=(P(("sens", "tm"), None), P(("sens", "tm"))),
        check_vma=False,
    )
```

time: 616 us -> 364 us (0.59); the launches traced: 607 us -> 363 us
  other arithmetic: 382 us -> 13.7 us
  Pallas kernels: 0 us -> 219 us
  blocking collectives: 131 us -> 60.3 us
  matrix products: 53.1 us -> 12.5 us
  waiting for transfers between devices: 19.4 us -> 34.3 us
    another operation x12 -> x0, other arithmetic: 368 us -> none  [the longest x4 188 us: solve_block(): lower_block = jnp.linalg.cholesky(moment_block)]
    pallas_call x0 -> x3, Pallas kernels: none -> 219 us  [the longest x2 206 us: invert(): pl.pallas_call(invert_kernel, out_shape=jax.ShapeDtypeStruct(a.shape, F32...]
    all_gather x9 -> x1, blocking collectives: 96.3 us -> 26.1 us  [per_device(): ends = lax.all_gather(mine, 'tm')]
    dot_general x6 -> x5, matrix products: 46.8 us -> 11.3 us  [the longest x1 6.86 us: per_device(): cross_terms = jnp.dot(observed, smoothed, preferred_element_type=F32)]
    psum x1, waiting for transfers between devices: 19.3 us -> 34.2 us  [per_device(): total = lax.psum(part, 'sens')]
  transfers between devices with their start and end apart: 4 -> 3, of which waited for: 1 -> 1; matrix products, arithmetic and copies ran while one was open for 66% -> 4% of each run, Pallas kernels for 0% -> 53%
where the time goes in v1:
time: 364 us; the launch traced here: 363 us
  Pallas kernels  219 us (60%)
  blocking collectives  60.3 us (17%)
  waiting for transfers between devices  34.3 us (9%)
  between operations  15.9 us (4%)
  other arithmetic  13.7 us (4%)
  matrix products  12.5 us (3%)
  local copies, waits for them, and re-layouts  7.24 us (2%)
    pallas_call x2, Pallas kernels, invert(): pl.pallas_call(invert_kernel, out_shape=jax.ShapeDtypeStruct(a.shape, F32...  206 us
    psum x1, waiting for transfers between devices, per_device(): total = lax.psum(part, 'sens')  34.2 us
    all_gather x1, blocking collectives, per_device(): all_moments = lax.all_gather(moment[None], 'tm', axis=0, tiled=True)  34.2 us
    all_gather x1, blocking collectives, per_device(): ends = lax.all_gather(mine, 'tm')  26.1 us
    pallas_call x1, Pallas kernels, info_and_gram(): pl.pallas_call(info_kernel, grid=(sensors // TILE,), in_specs=[pl.BlockSp...  13.2 us
    reduce_sum x1, other arithmetic, per_device(): sums_sq = jnp.sum(jnp.square(observed.astype(F32)), axis=1)  7.51 us
  transfers between devices with their start and end apart: 3, of which 1 were waited for; matrix products, arithmetic and copies ran while one was open for 4% of the time, Pallas kernels for 53%

profile of v1, /device:TPU:0, one launch (start us, length us, event | category | flops | bytes accessed | tf_op | source)
XLA Modules:
  0.0 363.3 jit_solution(7279862462779230306)
XLA Ops:
  7.2 0.0 all-reduce.68.cloned.1.call-start
  7.2 0.8 fusion.46
  8.1 0.6 fusion.3
  8.7 0.9 bitcast_divide_fusion
  9.6 0.0 copy-start
  9.6 3.4 copy-done
  13.0 0.0 copy-start.2
  13.0 13.2 %shard_map.68 = f32[128,384]{1,0:T(8,128)} custom-call(bf16[16384,256]{1,0:T(8,128)(2,1)S(1)} %copy-done, f32[16384,128]{1,0:T(8,128)} %load_ref.1, f32[1,16384]{1,0:T(1,128)S(1)} %bitcast.205), custom_call_target="tpu_custom_call" | custom-call | tf_op jit(solution)/shard_map/pallas_call | solution.py:41
  26.2 0.0 all-reduce.68.cloned.1.call-update
  26.2 0.0 reduce-scatter.2.cloned.1.call-start
  26.2 0.1 bitcast_convert_fusion
  26.3 0.0 copy-done.2
  26.5 34.2 %all-reduce.68.cloned.1.call-done = f32[128,384]{1,0:T(8,128)} async-done(((f32[128,384]{1,0:T(8,128)}), f32[128,384]{1,0:T(8,128)}) %all-reduce.68.cloned.1.call-update) | async-done | bytes 196624 | tf_op jit(solution)/shard_map/psum | solution.py:110
  60.8 0.9 fusion.13.a_ref
  61.6 12.7 %shard_map.69 = f32[1,128,128]{2,1,0:T(8,128)S(1)} custom-call(f32[1,128,128]{2,1,0:T(8,128)S(1)} %fusion.13.a_ref), custom_call_target="tpu_custom_call" | custom-call | tf_op jit(solution)/shard_map/pallas_call | solution.py:81
  74.3 1.3 fusion.9
  79.3 26.1 %all-gather.2 = f32[8,3,128]{2,1,0:T(4,128)S(1)} all-gather(f32[1,3,128]{2,1,0:T(4,128)S(1)} %maximum_bitcast_fusion), channel_id=2, replica_groups=mesh['sens'=4,'tm'=8] {'tm'}, dimensions={0}, use_global_device_ids=true | all-gather | bytes 13824 | tf_op jit(solution)/shard_map/all_gather | solution.py:123
  105.4 0.1 rev.10
  105.5 0.1 rev.9
  105.7 0.1 multiply_convert_fusion
  105.8 6.9 %fusion = f32[16384,128]{1,0:T(8,128)} fusion(bf16[256,128]{1,0:T(8,128)(2,1)S(1)} %multiply_convert_fusion, bf16[16384,256]{1,0:T(8,128)(2,1)} %obs_ref.1, bf16[16384]{0:T(1024)(128)(2,1)S(1)} %bitcast_convert_fusion), kind=kOutput, calls=%fused_computation.1 | convolution fusion | flops 1077936128 | bytes 16875520 | tf_op jit(solution)/shard_map/dot_general | solution.py:138
  112.6 0.0 copy-start.3
  112.6 0.0 reduce-scatter.2.cloned.1.call-update
  112.6 0.0 all-reduce.70.cloned.1.call-start
  112.7 7.5 %multiply_reduce_fusion = f32[16384]{0:T(1024)} fusion(bf16[16384,256]{1,0:T(8,128)(2,1)} %obs_ref.1, bf16[16384]{0:T(1024)(128)(2,1)S(1)} %bitcast_convert_fusion), kind=kLoop, calls=%fused_computation | loop fusion | flops 16760832 | bytes 8486912 | tf_op jit(solution)/shard_map/reduce_sum | solution.py:137
  120.2 0.0 all-reduce.70.cloned.1.call-update
  120.2 0.1 dynamic-slice_reduce_fusion
  120.3 0.0 copy-done.3
  120.3 0.6 dynamic-slice
  121.6 0.2 convolution_add_fusion
  121.8 34.2 %all-gather.1 = f32[1024,128]{1,0:T(8,128)S(1)} all-gather(f32[128,128]{1,0:T(8,128)S(1)} %convolution_add_fusion), channel_id=3, replica_groups=mesh['sens'=4,'tm'=8] {'tm'}, dimensions={0}, use_global_device_ids=true | all-gather | bytes 589824 | tf_op jit(solution)/shard_map/all_gather | solution.py:145
  156.0 1.2 fusion.7
  157.2 0.3 copy.8.a_ref
  157.5 193.5 %shard_map.70 = f32[16,128,128]{2,1,0:T(8,128)S(1)} custom-call(f32[16,128,128]{2,1,0:T(8,128)S(1)} %copy.8.a_ref), custom_call_target="tpu_custom_call" | custom-call | tf_op jit(solution)/shard_map/pallas_call | solution.py:81
  351.0 0.0 reduce-scatter.2.cloned.1.call-done
  351.0 2.4 fusion.54
  353.4 0.0 copy-start.1
  353.4 1.9 multiply_reduce_fusion.1
  355.4 0.0 all-reduce.70.cloned.1.call-done
  355.4 1.4 fusion.22
  356.8 0.0 copy-done.1
  (255 shorter events, 2.7 us)
Async XLA Ops:
  7.2 53.6 %all-reduce.68.cloned.1.call-start = ((), (), s32[]{:S(2)}) async-start(), calls=%async_computation.1 | async-start | bytes 393216 | tf_op jit(solution)/shard_map/psum | solution.py:110
  9.6 3.4 copy-start
  13.0 13.3 %copy-start.2 = (f32[256,128]{1,0:T(8,128)S(1)}, f32[256,128]{1,0:T(8,128)}, u32[]{:S(2)}) copy-start(f32[256,128]{1,0:T(8,128)} %param.8) | copy-start | bytes 393220
  26.2 324.8 %reduce-scatter.2.cloned.1.call-start = ((), (), s32[]{:S(2)}) async-start(), calls=%async_computation.2 | async-start | bytes 9437184 | tf_op jit(solution)/shard_map/reduce_scatter | solution.py:143
  112.6 7.7 %copy-start.3 = (u32[32]{0:T(128)S(1)}, u32[32]{0:T(128)}, u32[]{:S(2)}) copy-start(u32[32]{0:T(128)} %constant.171) | copy-start | bytes 388
  112.6 242.8 %all-reduce.70.cloned.1.call-start = ((), (), s32[]{:S(2)}) async-start(), calls=%async_computation.3 | async-start | bytes 131072
  353.4 3.4 copy-start.1
Sparse Core Ops, SparseCore 0:
  26.3 34.4 all-reduce.67
  112.8 151.9 reduce-scatter.1
  268.2 67.9 all-reduce.69
